TPU v7x, 32 devices: a whole 2x2x4 slice. The times are simulated.
32 devices in a mesh: slide: 2 (over x), row: 16 (over z, y, core).
Axes of the slice: x: 2, y: 2, z: 4, core: 2. Of those that a mesh axis runs over, the one named last changes fastest.
Arguments:
- tokens: bfloat16 [128, 128, 768], P(('slide', 'row')), parts along dimension 0, may hold values from -6 to 6
- norm_gain: float32 [768], replicated, may hold values from 0.1 to 1.9
- query_weight: bfloat16 [768, 768], replicated, may hold values from -0.875 to 0.875
- key_weight: bfloat16 [768, 768], replicated, may hold values from -0.875 to 0.875
- value_weight: bfloat16 [768, 768], replicated, may hold values from -0.21875 to 0.21875
- out_weight: bfloat16 [768, 768], replicated, may hold values from -0.21875 to 0.21875
- head_scale: float32 [12], replicated, may hold values from 0.02 to 0.5
- pool_queries: bfloat16 [16, 768], replicated, may hold values from -24 to 24
Outputs:
- mixed: bfloat16 [128, 128, 768], P(('slide', 'row')), parts along dimension 0
- pooled: float32 [32, 768], P('slide'), parts along dimension 0
There are 2 independent parts, one for each index of `slide`. A program takes and returns all parts, laid end to end along the dimension named above; an argument that names none is the same for every part. Nothing has to cross between parts.
All inputs are finite; a program needn't handle non-finite values.
Results may differ from a plain program's by a relative error of at most 0.007.
The roundings to bfloat16 on the way count: a program that leaves them out, or rounds other values in their place, can miss the bound.
Values may be sent and summed in bfloat16 or wider, within the bound.
A program may use at most 128 MiB of HBM per device.

v0:
```python
import jax
import jax.numpy as jnp
from jax import lax
from jax.sharding import PartitionSpec as P

RAD = 4


norm_eps = 1e-06


def extended(cells, sides, width):
    for axis, dim in sides:
        count = lax.axis_size(axis)
        ends = count - 1
        head = lax.slice_in_dim(cells, 0, width, axis=dim)
        tail = lax.slice_in_dim(cells, cells.shape[dim] - width, cells.shape[dim], axis=dim)
        cells = jnp.concatenate(
            [
                lax.ppermute(tail, axis, [(i, (i + 1) % count) for i in range(ends)]),
                cells,
                lax.ppermute(head, axis, [((i + 1) % count, i) for i in range(ends)]),
            ],
            axis=dim,
        )
    return cells


def merged_2(shard, axis, combine):
    everything = jax.tree.map(lambda part: lax.all_gather(part, axis), shard)
    initial = jax.tree.map(lambda part: part[0], everything)

    def hop(k, so_far):
        return combine(so_far, jax.tree.map(lambda part: part[k], everything))

    return lax.fori_loop(1, lax.axis_size(axis), hop, initial)


def normalize(tokens, norm_gain):
    feats = tokens.astype(jnp.float32)
    mean_sq = jnp.mean(feats * feats, axis=-1, keepdims=True)
    return (feats * lax.rsqrt(mean_sq + norm_eps) * norm_gain).astype(jnp.bfloat16)


def project(weight, normed, head_count):
    row_count, col_count, feature_width = normed.shape
    flattened = normed.reshape(row_count * col_count, feature_width)
    projected = lax.dot_general(
        weight, flattened, (((0,), (1,)), ((), ())), preferred_element_type=jnp.float32
    )
    return projected.astype(jnp.bfloat16).reshape(
        head_count, feature_width // head_count, row_count, col_count
    )


def lorentz_time(spatial):
    spatial_f = spatial.astype(jnp.float32)
    return jnp.sqrt(1.0 + jnp.sum(spatial_f * spatial_f, axis=1))


def split_cols(array, group, block, reach):
    blocks = group // block
    lead = array.shape[:-1]
    main_part = array[..., :group].reshape(lead + (blocks, block))
    extra = array[..., block:]
    pad_width = [(0, 0)] * len(lead) + [(0, blocks * block - extra.shape[-1])]
    extra = jnp.pad(extra, pad_width).reshape(lead + (blocks, block))[..., : 2 * reach]
    return jnp.concatenate([main_part, extra], axis=-1)


def window_attend(query_heads, key_rows, value_rows, row_inside, head_scale):
    head_count, head_width, row_count, col_count = query_heads.shape
    group = 128
    block = 32
    blocks = group // block
    tile_rows = 4
    key_tile_rows = tile_rows + 2 * RAD
    key_tile_cols = block + 2 * RAD
    key_pad = jnp.pad(key_rows, ((0, 0), (0, 0), (0, 0), (RAD, RAD)))
    value_pad = jnp.pad(value_rows, ((0, 0), (0, 0), (0, 0), (RAD, RAD)))
    key_time = lorentz_time(key_pad)
    value_time = lorentz_time(value_pad)
    query_time = lorentz_time(query_heads)
    col_global = jnp.arange(col_count + 2 * RAD, dtype=jnp.int32) - RAD
    col_inside = (col_global >= 0) & (col_global < col_count)
    query_row = jnp.arange(tile_rows, dtype=jnp.int32)[:, None, None, None]
    query_col = jnp.arange(block, dtype=jnp.int32)[None, :, None, None]
    key_row = jnp.arange(key_tile_rows, dtype=jnp.int32)[None, None, :, None]
    key_col = jnp.arange(key_tile_cols, dtype=jnp.int32)[None, None, None, :]
    row_gap = key_row - query_row
    col_gap = key_col - query_col
    window_mask = (row_gap >= 0) & (row_gap <= 2 * RAD) & (col_gap >= 0) & (col_gap <= 2 * RAD)
    window_mask = window_mask.reshape(tile_rows * block, key_tile_rows * key_tile_cols)
    col_groups = col_count // group
    tile_count = row_count // tile_rows * col_groups

    def one_tile(tile_index):
        query_blocks = query_heads.reshape(head_count, head_width, tile_rows, blocks, block)
        query_blocks = query_blocks.transpose(0, 3, 1, 2, 4).reshape(
            head_count, blocks, head_width, tile_rows * block
        )
        key_blocks = split_cols(key_pad, group, block, RAD).transpose(0, 3, 1, 2, 4)
        key_blocks = key_blocks.reshape(
            head_count, blocks, head_width, key_tile_rows * key_tile_cols
        )
        value_blocks = split_cols(value_pad, group, block, RAD).transpose(0, 3, 1, 2, 4)
        value_blocks = value_blocks.reshape(
            head_count, blocks, head_width, key_tile_rows * key_tile_cols
        )
        qtime_blocks = query_time.reshape(head_count, tile_rows, blocks, block).transpose(
            0, 2, 1, 3
        )
        qtime_blocks = qtime_blocks.reshape(head_count, blocks, tile_rows * block)
        ktime_blocks = split_cols(key_time, group, block, RAD).transpose(0, 2, 1, 3)
        ktime_blocks = ktime_blocks.reshape(head_count, blocks, key_tile_rows * key_tile_cols)
        vtime_blocks = split_cols(value_time, group, block, RAD).transpose(0, 2, 1, 3)
        vtime_blocks = vtime_blocks.reshape(head_count, blocks, key_tile_rows * key_tile_cols)
        cin_blocks = split_cols(col_inside, group, block, RAD)
        key_valid = row_inside[:, None, None] & cin_blocks[None]
        key_valid = key_valid.transpose(1, 0, 2).reshape(blocks, key_tile_rows * key_tile_cols)
        inner = jnp.einsum(
            "hbdq,hbdk->hbqk", query_blocks, key_blocks, preferred_element_type=jnp.float32
        )
        lorentz_dot = inner - qtime_blocks[:, :, :, None] * ktime_blocks[:, :, None, :]
        scores_now = head_scale[:, None, None, None] * (2.0 + 2.0 * lorentz_dot)
        allowed = window_mask[None, None] & key_valid[None, :, None, :]
        scores_now = jnp.where(allowed, scores_now, -jnp.inf)
        peak_score = jnp.max(scores_now, axis=-1, keepdims=True)
        weights = jnp.exp(scores_now - peak_score).astype(jnp.bfloat16)
        mean_space = jnp.einsum(
            "hbqk,hbdk->hbdq", weights, value_blocks, preferred_element_type=jnp.float32
        )
        mean_time = jnp.sum(weights.astype(jnp.float32) * vtime_blocks[:, :, None, :], axis=-1)
        spread = jnp.sqrt(mean_time * mean_time - jnp.sum(mean_space * mean_space, axis=2))
        attended = (mean_space / spread[:, :, None, :]).astype(jnp.bfloat16)
        attended = attended.reshape(head_count, blocks, head_width, tile_rows, block).transpose(
            0, 2, 3, 1, 4
        )
        return attended.reshape(head_count, head_width, tile_rows, group)

    tiles = lax.map(one_tile, jnp.arange(tile_count, dtype=jnp.int32))
    tiles = tiles.reshape(
        row_count // tile_rows, col_groups, head_count, head_width, tile_rows, group
    )
    return tiles.transpose(2, 3, 0, 4, 1, 5).reshape(head_count, head_width, row_count, col_count)


def mix_out(attended, out_weight, token_block):
    head_count, head_width, row_count, col_count = attended.shape
    flattened = attended.reshape(head_count * head_width, row_count * col_count)
    projected = lax.dot_general(
        flattened, out_weight, (((0,), (0,)), ((), ())), preferred_element_type=jnp.float32
    )
    projected = projected.reshape(row_count, col_count, head_count * head_width)
    return (token_block.astype(jnp.float32) + projected).astype(jnp.bfloat16)


def pool_scores(pool_queries, key_heads, head_scale):
    head_count, head_width = (key_heads.shape[0], key_heads.shape[1])
    key_flat = key_heads.reshape(head_count, head_width, -1)
    pool_space = pool_queries.astype(jnp.float32).reshape(
        pool_queries.shape[0], head_count, head_width
    )
    pool_time = jnp.sqrt(1.0 + jnp.sum(pool_space * pool_space, axis=-1))
    lorentz_dot = jnp.einsum(
        "phd,hdt->pht", pool_space, key_flat.astype(jnp.float32), precision=lax.Precision.HIGHEST
    )
    lorentz_dot = lorentz_dot - pool_time[:, :, None] * lorentz_time(key_flat)[None]
    return head_scale[None, :, None] * (2.0 + 2.0 * lorentz_dot)


def pool_partial(pool_score, peak_score, value_heads):
    head_count, head_width = (value_heads.shape[0], value_heads.shape[1])
    value_flat = value_heads.reshape(head_count, head_width, -1)
    weights = jnp.exp(pool_score - peak_score[:, :, None])
    mean_space = jnp.einsum(
        "pht,hdt->phd", weights, value_flat.astype(jnp.float32), precision=lax.Precision.HIGHEST
    )
    mean_time = jnp.sum(weights * lorentz_time(value_flat)[None], axis=-1)
    return (mean_space, mean_time)


def combine_pools(earlier_part, later_part):
    peak_score = jnp.maximum(earlier_part[0], later_part[0])
    factor_early = jnp.exp(earlier_part[0] - peak_score)
    factor_late = jnp.exp(later_part[0] - peak_score)
    mean_space = (
        earlier_part[1] * factor_early[:, :, None] + later_part[1] * factor_late[:, :, None]
    )
    mean_time = earlier_part[2] * factor_early + later_part[2] * factor_late
    return (peak_score, mean_space, mean_time)


def per_device(
    tokens, norm_gain, query_weight, key_weight, value_weight, out_weight, head_scale, pool_queries
):
    row_count, col_count, feature_width = tokens.shape
    head_count = head_scale.shape[0]
    normed = normalize(tokens, norm_gain)
    query_heads = project(query_weight, normed, head_count)
    key_heads = project(key_weight, normed, head_count)
    value_heads = project(value_weight, normed, head_count)
    stacked_rims = extended(jnp.stack([key_heads, value_heads]), (("row", 3),), RAD)
    key_rows = stacked_rims[0]
    value_rows = stacked_rims[1]
    total_rows = row_count * lax.axis_size("row")
    global_rows = (
        lax.axis_index("row") * row_count - RAD + jnp.arange(row_count + 2 * RAD, dtype=jnp.int32)
    )
    row_inside = (global_rows >= 0) & (global_rows < total_rows)
    attended = window_attend(query_heads, key_rows, value_rows, row_inside, head_scale)
    mixed = mix_out(attended, out_weight, tokens)
    pool_score = pool_scores(pool_queries, key_heads, head_scale)
    local_peak = jnp.max(pool_score, axis=-1)
    mean_space, mean_time = pool_partial(pool_score, local_peak, value_heads)
    merged = merged_2((local_peak, mean_space, mean_time), "row", combine_pools)
    mean_space = merged[1]
    mean_time = merged[2]
    spread = jnp.sqrt(mean_time * mean_time - jnp.sum(mean_space * mean_space, axis=-1))
    pooled = (mean_space / spread[:, :, None]).reshape(mean_space.shape[0], feature_width)
    return (mixed, pooled)


def solution(mesh):
    placed = (P(("slide", "row"), None, None), P(), P(), P(), P(), P(), P(), P())
    return jax.shard_map(
        per_device,
        mesh=mesh,
        in_specs=placed,
        out_specs=(P(("slide", "row"), None, None), P("slide", None)),
        check_vma=False,
    )
```

profile of v0, /device:TPU:0, one launch (start us, length us, event | category | flops | bytes accessed | tf_op | source)
XLA Modules:
  0.0 231.4 jit_solution(14739717786627771079)
XLA Ops:
  0.6 1.5 fusion.5
  2.1 1.4 fusion.7
  3.5 2.3 %fusion.10 = bf16[768,512]{0,1:T(8,128)(2,1)S(1)} fusion(bf16[512,768]{1,0:T(8,128)(2,1)S(1)} %bitcast.115, bf16[768,768]{1,0:T(8,128)(2,1)} %param.14), kind=kOutput, calls=%fused_computation.41 | convolution fusion | flops 604372992 | bytes 2752512 | tf_op jit(solution)/shard_map/dot_general | solution.py:48
  6.3 2.9 %fusion.9 = bf16[768,512]{0,1:T(8,128)(2,1)} fusion(bf16[512,768]{1,0:T(8,128)(2,1)S(1)} %bitcast.116, bf16[768,768]{1,0:T(8,128)(2,1)} %param.13), kind=kOutput, calls=%fused_computation.40 | convolution fusion | flops 604372992 | bytes 2752512 | tf_op jit(solution)/shard_map/dot_general | solution.py:48
  9.3 1.4 copy.94
  10.7 1.1 stack_reshape.6
  11.7 2.4 %constant_dynamic-update-slice_fusion.1 = bf16[2,12,64,4,128]{4,3,2,1,0:T(4,128)(2,1)} fusion(bf16[1,12,64,4,128]{4,3,2,1,0:T(4,128)(2,1)} %stack_reshape.6), kind=kLoop, calls=%fused_computation.77 | loop fusion | bytes 1572864
  14.1 1.2 constant_dynamic-update-slice_fusion
  15.3 1.3 collective-permute-start.1
  16.6 4.2 %collective-permute-start = (bf16[2,12,64,4,128]{4,3,2,1,0:T(4,128)(2,1)}, bf16[2,12,64,4,128]{4,3,2,1,0:T(4,128)(2,1)}, u32[]{:S(2)}, u32[]{:S(2)}) collective-permute-start(bf16[2,12,64,4,128]{4,3,2,1,0:T(4,128)(2,1)} %constant_dynamic-update-slice_fusion), channel_id=1, source_target_pairs={{0,1},{1,2},{2,3},{3,4},{4,5},{5,6},{6,7},{7,8},{8,9},{9,10},{10,1... | collective-permute-start | bytes 4718600 | tf_op jit(solution)/shard_map/ppermute | solution.py:20
  23.0 1.0 and.116
  26.0 40.5 %all-gather.2 = f32[256,12]{1,0:T(8,128)S(1)} all-gather(f32[16,12]{1,0:T(8,128)S(1)} %copy.117), channel_id=4, replica_groups=mesh['slide'=2,'row'=16] {'row'}, dimensions={0}, use_global_device_ids=true | all-gather | bytes 13056 | tf_op jit(solution)/shard_map/all_gather | solution.py:30
  66.5 21.0 %all-gather = f32[256,12]{1,0:T(8,128)S(1)} all-gather(f32[16,12]{1,0:T(8,128)S(1)} %copy.115), channel_id=2, replica_groups=mesh['slide'=2,'row'=16] {'row'}, dimensions={0}, use_global_device_ids=true | all-gather | bytes 13056 | tf_op jit(solution)/shard_map/all_gather | solution.py:30
  87.5 25.4 %all-gather.1 = f32[256,12,64]{2,0,1:T(8,128)S(1)} all-gather(f32[16,12,64]{2,0,1:T(8,128)S(1)} %convolution_bitcast_fusion.1), channel_id=3, replica_groups=mesh['slide'=2,'row'=16] {'row'}, dimensions={0}, use_global_device_ids=true | all-gather | bytes 835584 | tf_op jit(solution)/shard_map/all_gather | solution.py:30
  113.0 1.1 copy-done.5
  114.1 16.8 %while.23 = (s32[]{:T(128)}, f32[16,12]{1,0:T(8,128)S(1)}, f32[16,12,64]{2,1,0:T(8,128)S(1)}, f32[16,12]{1,0:T(8,128)S(1)}, f32[16,16,12]{2,1,0:T(8,128)S(1)}, /...) while((s32[]{:T(128)}, f32[16,12]{1,0:T(8,128)S(1)}, ...), condition=%wide.region_13.14_spmd, body=%wide.region_12.13_spmd.sunk | while | flops 38021 | bytes 253583 | solution.py:36
  114.1 0.9 constant_dynamic-slice_fusion.2
  115.2 0.9 constant_dynamic-slice_fusion.2
  116.3 0.9 constant_dynamic-slice_fusion.2
  118.6 0.9 constant_dynamic-slice_fusion.2
  119.7 0.9 constant_dynamic-slice_fusion.2
  131.9 1.7 convert_multiply_fusion.2
  133.5 1.6 copy.105
  135.2 1.9 mul.230
  137.6 1.3 reshape_reshape.10
  138.8 1.6 copy.99
  140.8 5.0 %pad_maximum_fusion = bf16[2,12,64,12,128]{4,3,2,1,0:T(8,128)(2,1)S(1)} fusion(bf16[2,12,64,4,128]{4,3,2,1,0:T(4,128)(2,1)} %collective-permute-done.1, bf16[2,12,64,4,128]{4,3,2,1,0:T(4,128)(2,1)} %constant_dynamic-update-slice_fusion, bf16[2,12,64,4,128]{4,3,2,1,0:T(4,128)(2,1)} %collective-permute-done), kind=kLoop, calls=%fused_computation.20 | loop fusion | flops 14155776 | bytes 9437184 | tf_op jit(solution)/shard_map/concatenate | solution.py:18
  145.8 1.7 slice_bitcast_fusion
  147.5 5.6 %multiply_reduce_fusion = (f32[12,12,136]{2,1,0:T(8,128)S(1)}, f32[12,12,136]{2,1,0:T(8,128)S(1)}) fusion(bf16[12,64,12,128]{3,2,1,0:T(8,128)(2,1)S(1)} %get-tuple-element.273, bf16[12,64,12,128]{3,2,1,0:T(8,128)(2,1)S(1)} %get-tuple-element.272), kind=kLoop, calls=%fused_computation.10 | loop fusion | flops 7481088 | bytes 4875264 | tf_op jit(solution)/shard_map/reduce_sum | solution.py:58
  153.4 3.8 %pad_slice_fusion = (bf16[12,64,12,104]{3,2,1,0:T(8,128)(2,1)}, bf16[12,64,12,104]{3,2,1,0:T(8,128)(2,1)}) fusion(bf16[12,64,12,128]{3,2,1,0:T(8,128)(2,1)S(1)} %get-tuple-element.272, bf16[12,64,12,128]{3,2,1,0:T(8,128)(2,1)S(1)} %get-tuple-element.273), kind=kLoop, calls=%fused_computation.15 | loop fusion | bytes 8552448 | tf_op jit(solution)/shard_map/while/body/eval_jaxpr/slice | solution.py:65
  157.2 3.8 %pad_slice_fusion.1 = (bf16[12,64,12,128]{3,2,1,0:T(8,128)(2,1)}, bf16[12,64,12,128]{3,2,1,0:T(8,128)(2,1)}) fusion(bf16[12,64,12,128]{3,2,1,0:T(8,128)(2,1)S(1)} %get-tuple-element.272, bf16[12,64,12,128]{3,2,1,0:T(8,128)(2,1)S(1)} %get-tuple-element.273), kind=kLoop, calls=%fused_computation.16 | loop fusion | bytes 9437184 | tf_op jit(solution)/shard_map/while/body/eval_jaxpr/slice | solution.py:64
  162.6 6.4 %copy.125 = bf16[12,64,12,104]{1,3,2,0:T(8,128)(2,1)} copy(bf16[12,64,12,104]{3,2,1,0:T(8,128)(2,1)} %get-tuple-element.284) | data formatting | bytes 3833856
  169.0 3.2 %pad.34.clone = bf16[12,64,12,128]{1,3,2,0:T(8,128)(2,1)S(1)} pad(bf16[12,64,12,104]{1,3,2,0:T(8,128)(2,1)} %copy.125, bf16[]{:T(256)} %constant.84.clone.1), padding=0_0x0_0x0_0x0_24 | pad | bytes 4276226 | tf_op jit(solution)/shard_map/while/body/eval_jaxpr/jit(_pad)/pad | solution.py:67
  172.5 6.5 %copy.100 = bf16[12,64,12,128]{1,3,2,0:T(8,128)(2,1)} copy(bf16[12,64,12,128]{3,2,1,0:T(8,128)(2,1)} %get-tuple-element.286) | data formatting | bytes 4718592 | tf_op jit(solution)/shard_map/while/body/eval_jaxpr/slice | solution.py:64
  179.0 3.9 %maximum_bitcast_fusion.1 = bf16[12,4,64,12,40]{2,4,1,3,0:T(8,128)(2,1)S(1)} fusion(bf16[12,64,12,4,8]{1,4,3,2,0:T(8,128)(2,1)S(1)} %slice.101, bf16[12,64,12,4,32]{1,4,3,2,0:T(8,128)(2,1)} %bitcast.102), kind=kLoop, calls=%fused_computation.22 | loop fusion | flops 5898240 | bytes 5898240 | tf_op jit(solution)/shard_map/while/body/eval_jaxpr/transpose | solution.py:102
  183.0 3.6 %copy.102 = bf16[12,4,64,12,40]{2,4,3,1,0:T(8,128)(2,1)} copy(bf16[12,4,64,12,40]{2,4,1,3,0:T(8,128)(2,1)S(1)} %maximum_bitcast_fusion.1) | data formatting | bytes 5898240 | tf_op jit(solution)/shard_map/while/body/eval_jaxpr/transpose | solution.py:102
  186.6 6.2 %copy.124 = bf16[12,64,12,104]{1,3,2,0:T(8,128)(2,1)} copy(bf16[12,64,12,104]{3,2,1,0:T(8,128)(2,1)} %get-tuple-element.285) | data formatting | bytes 3833856
  192.8 3.2 %pad.31.clone = bf16[12,64,12,128]{1,3,2,0:T(8,128)(2,1)S(1)} pad(bf16[12,64,12,104]{1,3,2,0:T(8,128)(2,1)} %copy.124, bf16[]{:T(256)} %constant.84.clone.1), padding=0_0x0_0x0_0x0_24 | pad | bytes 4276226 | tf_op jit(solution)/shard_map/while/body/eval_jaxpr/jit(_pad)/pad | solution.py:67
  196.3 6.5 %copy.96 = bf16[12,64,12,128]{1,3,2,0:T(8,128)(2,1)} copy(bf16[12,64,12,128]{3,2,1,0:T(8,128)(2,1)} %get-tuple-element.287) | data formatting | bytes 4718592 | tf_op jit(solution)/shard_map/while/body/eval_jaxpr/slice | solution.py:64
  202.8 4.1 %maximum_bitcast_fusion = bf16[12,4,64,12,40]{2,4,1,3,0:T(8,128)(2,1)S(1)} fusion(bf16[12,64,12,4,8]{1,4,3,2,0:T(8,128)(2,1)S(1)} %slice.99, bf16[12,64,12,4,32]{1,4,3,2,0:T(8,128)(2,1)} %bitcast.103), kind=kLoop, calls=%fused_computation.21 | loop fusion | flops 5898240 | bytes 5898240 | tf_op jit(solution)/shard_map/while/body/eval_jaxpr/transpose | solution.py:106
  206.9 1.0 copy.98
  208.8 3.7 %fusion.4 = (f32[12,4,128]{2,1,0:T(4,128)S(1)}, f32[12,4,128,480]{2,3,1,0:T(8,128)S(1)}) fusion(f32[12,4,480]{2,1,0:T(4,128)S(1)} %mul.234, f32[12,4,128]{2,1,0:T(4,128)S(1)} %mul.231, f32[12]{0:T(128)S(1)} %copy-done.10, pred[4,128,480]{1,2,0:T(8,128)(4,1)S(1)} %broadcast_and_fusion, bf16[12,4,64,128]{2,3,1,0:T(8,128)(2,1)S(1)} %bitcast.119, ...), kind=kOutput, calls=%fused_computation.19 | convolution fusion | flops 398125056 | bytes 15919152 | tf_op jit(solution)/shard_map/while/body/eval_jaxpr/hbdq,hbdk->hbqk/dot_general | solution.py:121
  212.5 7.3 %multiply_reduce_fusion.2 = (f32[12,4,128]{2,1,0:T(4,128)S(1)}, bf16[12,4,128,480]{2,3,1,0:T(8,128)(2,1)S(1)}) fusion(f32[12,4,480]{2,1,0:T(4,128)S(1)} %mul.240, f32[12,4,128]{2,1,0:T(4,128)S(1)} %get-tuple-element.276, f32[12,4,128,480]{2,3,1,0:T(8,128)S(1)} %get-tuple-element.277, f32[12,4,480]{2,1,0:T(4,128)S(1)} %mul.234, f32[12,4,128]{2,1,0:T(4,128)S(1)} %mul.231, ...), kind=kLoop, calls=%fused_computation.12 | loop fusion | flops 32434176 | bytes 18198576 | tf_op jit(solution)/shard_map/while/body/eval_jaxpr/reduce_sum | solution.py:133
  219.8 1.8 multiply_reduce_fusion.5
  221.8 1.6 copy.110
  223.4 2.6 %copy.111 = bf16[12,64,4,4,32]{1,0,4,3,2:T(8,128)(2,1)S(1)} copy(bf16[12,64,4,4,32]{1,4,2,3,0:T(8,128)(2,1)} %bitcast.111) | data formatting | bytes 1572864 | tf_op jit(solution)/shard_map/while/body/eval_jaxpr/transpose | solution.py:136
  226.0 2.0 reshape_reshape_transpose_reshape.3
  228.0 3.4 %fusion.8 = bf16[4,128,768]{2,1,0:T(8,128)(2,1)} fusion(bf16[4,128,768]{2,1,0:T(8,128)(2,1)} %param.10, bf16[4,128,768]{2,1,0:T(8,128)(2,1)} %bitcast.122, bf16[768,768]{1,0:T(8,128)(2,1)} %param.15), kind=kOutput, calls=%fused_computation.31 | convolution fusion | flops 605159424 | bytes 3538944 | tf_op jit(solution)/shard_map/dot_general | solution.py:151
  (138 shorter events, 21.7 us)
Async XLA Ops:
  0.6 131.2 %copy-start = (bf16[768,768]{1,0:T(8,128)(2,1)S(1)}, bf16[768,768]{1,0:T(8,128)(2,1)}, u32[]{:S(2)}) copy-start(bf16[768,768]{1,0:T(8,128)(2,1)} %param.12) | copy-start | bytes 3538948
  3.5 2.8 %copy-start.2 = (bf16[4,128,768]{2,1,0:T(8,128)(2,1)}, bf16[4,128,768]{2,1,0:T(8,128)(2,1)S(1)}, u32[]{:S(2)}) copy-start(bf16[4,128,768]{2,1,0:T(8,128)(2,1)S(1)} %fusion.7) | copy-start | bytes 2359300
  11.7 9.1 %copy-start.9 = (bf16[16,768]{1,0:T(8,128)(2,1)S(1)}, bf16[16,768]{1,0:T(8,128)(2,1)}, u32[]{:S(2)}) copy-start(bf16[16,768]{1,0:T(8,128)(2,1)} %param.17) | copy-start | bytes 73732
  11.7 12.7 %copy-start.10 = (f32[12]{0:T(128)S(1)}, f32[12]{0:T(128)}, u32[]{:S(2)}) copy-start(f32[12]{0:T(128)} %param.16) | copy-start | bytes 148
  15.3 125.4 %collective-permute-start.1 = (bf16[2,12,64,4,128]{4,3,2,1,0:T(4,128)(2,1)}, bf16[2,12,64,4,128]{4,3,2,1,0:T(4,128)(2,1)}, u32[]{:S(2)}, u32[]{:S(2)}) collective-permute-start(bf16[2,12,64,4,128]{4,3,2,1,0:T(4,128)(2,1)} %constant_dynamic-update-slice_fusion), channel_id=1, source_target_pairs={{1,0},{2,1},{3,2},{4,3},{5,4},{6,5},{7,6},{8,7},{9,8},{10,9},{11,1... | collective-permute-start | bytes 4718600 | tf_op jit(solution)/shard_map/ppermute | solution.py:22
  16.6 124.2 %collective-permute-start = (bf16[2,12,64,4,128]{4,3,2,1,0:T(4,128)(2,1)}, bf16[2,12,64,4,128]{4,3,2,1,0:T(4,128)(2,1)}, u32[]{:S(2)}, u32[]{:S(2)}) collective-permute-start(bf16[2,12,64,4,128]{4,3,2,1,0:T(4,128)(2,1)} %constant_dynamic-update-slice_fusion), channel_id=1, source_target_pairs={{0,1},{1,2},{2,3},{3,4},{4,5},{5,6},{6,7},{7,8},{8,9},{9,10},{10,1... | collective-permute-start | bytes 4718600 | tf_op jit(solution)/shard_map/ppermute | solution.py:20
  66.5 65.4 %copy-start.3 = (bf16[4,128,768]{2,1,0:T(8,128)(2,1)S(1)}, bf16[4,128,768]{2,1,0:T(8,128)(2,1)}, u32[]{:S(2)}) copy-start(bf16[4,128,768]{2,1,0:T(8,128)(2,1)} %copy-done.2) | copy-start | bytes 2359300
  112.9 1.1 copy-start.5
  135.2 2.4 %copy-start.4 = (bf16[768,512]{0,1:T(8,128)(2,1)S(1)}, bf16[768,512]{0,1:T(8,128)(2,1)}, u32[]{:S(2)}) copy-start(bf16[768,512]{0,1:T(8,128)(2,1)} %get-tuple-element.275) | copy-start | bytes 2359300
  137.5 2.9 %copy-start.8 = (pred[128,480]{0,1:T(8,128)(4,1)S(1)}, pred[128,480]{0,1:T(8,128)(4,1)}, u32[]{:S(2)}) copy-start(pred[128,480]{0,1:T(8,128)(4,1)} %and.116) | copy-start | bytes 184324
  153.1 4.1 %copy-start.7 = (f32[12,12,136]{2,1,0:T(8,128)}, f32[12,12,136]{2,1,0:T(8,128)S(1)}, u32[]{:S(2)}) copy-start(f32[12,12,136]{2,1,0:T(8,128)S(1)} %add_sqrt_fusion) | copy-start | bytes 235012
  160.9 1.0 slice-start.2
  202.8 5.2 %slice-start = ((s8[5898240]{0:T(1024)(128)(4,1)}), s8[4194304]{0:T(1024)(128)(4,1)S(1)}, s32[]{:S(2)}) async-start(s8[5898240]{0:T(1024)(128)(4,1)} %bitcast.112), calls=%async_computation | async-start | bytes 8388608
  206.9 1.5 slice-start.1
  206.9 1.9 copy-start.6
  223.4 8.0 %copy-start.1 = (bf16[768,768]{1,0:T(8,128)(2,1)S(1)}, bf16[768,768]{1,0:T(8,128)(2,1)}, u32[]{:S(2)}) copy-start(bf16[768,768]{1,0:T(8,128)(2,1)} %param.12) | copy-start | bytes 3538948
where the time goes:
time: 233 us; the launch traced here: 231 us
  blocking collectives  87 us (37%)
  local copies, waits for them, and re-layouts  86.1 us (37%)
  other arithmetic  34.2 us (15%)
  matrix products  16.9 us (7%)
  starting transfers between devices  5.49 us (2%)
    all_gather x3, blocking collectives, merged_2(): everything = jax.tree.map(lambda part: lax.all_gather(part, axis), shard)  87 us
    unnamed x29, local copies, waits for them, and re-layouts  16.9 us
    slice x6, local copies, waits for them, and re-layouts, split_cols(): main_part = array[..., :group].reshape(lead + (blocks, block))  16.8 us
    dynamic_slice x15, local copies, waits for them, and re-layouts, hop(): return combine(so_far, jax.tree.map(lambda part: part[k], everything))  13.7 us
    reduce_sum x1, other arithmetic, one_tile(): jnp.sum(weights.astype(jnp.float32) * vtime_blocks[:, :, None, :], axis=-1)  7.33 us
    dot_general x3, matrix products, project(): lax.dot_general(weight, flattened, (((0,), (1,)), ((), ())), preferred_el...  6.92 us
    pad x5, local copies, waits for them, and re-layouts, split_cols(): jnp.pad(extra, pad_width).reshape(lead + (blocks, block))[..., :2 * reach]  6.4 us
    reduce_sum x4, other arithmetic, lorentz_time(): return jnp.sqrt(1.0 + jnp.sum(spatial_f * spatial_f, axis=1))  6.17 us
  transfers between devices with their start and end apart: 2, of which 0 were waited for; matrix products, arithmetic and copies ran while one was open for 13% of the time, Pallas kernels for 0%

commit v1 on v0

v1 whole, which is shorter than its diff:
```python
import functools
import math

import jax
import jax.numpy as jnp
import numpy as np
from jax import lax
from jax.experimental import pallas as pl
from jax.experimental.pallas import tpu as pltpu
from jax.sharding import PartitionSpec as P

RAD = 4
EPS = 1e-06
PAD = 8
BLOCK = 32
WIN = BLOCK + 2 * PAD
RING = 48
LOG2E = math.log2(math.e)
FAR = -(2.0**30)
MESH = pl.DeviceIdType.MESH
BF = jnp.bfloat16
F32 = jnp.float32
NT = (((1,), (1,)), ((), ()))


def tables(heads, width, rows, cols):
    hw = width // heads
    t6, t3 = 6 * heads, 3 * heads
    row0, col0 = t6, t6 + rows
    pool_lane = col0 + RING
    assert pool_lane < 128
    lane = np.arange(128)
    head_of = np.arange(width) // hw
    ek = ((lane[None] // 6 == head_of[:, None]) & (lane[None] < t6)).astype(np.float32)
    ev = ((lane[None] // 3 == head_of[:, None]) & (lane[None] < t3)).astype(np.float32)
    sel = np.full((8, 128), 3.0, np.float32)
    sel[0, :t6] = np.tile([0, 1, 0, 1, 2, 0], heads)
    sel[1, :t6] = np.tile([0, 0, 1, 1, 0, 2], heads)
    sel[2, :t3] = np.tile([0, 1, 2], heads)
    pc = np.arange(cols + 2 * PAD) - PAD
    inside = (pc >= 0) & (pc < cols)
    kcol = np.zeros((cols + 2 * PAD, 128), np.float32)
    m = np.arange(RING)
    near = ((pc[:, None] - m[None] + RAD) % RING <= 2 * RAD) & inside[:, None]
    kcol[:, col0 : col0 + RING] = np.where(near, 0.0, FAR)
    kcol[:, pool_lane] = np.where(inside, 0.0, FAR)
    qcol = np.zeros((cols, 128), np.float32)
    qcol[np.arange(cols), col0 + np.arange(cols) % RING] = 1.0
    return (
        jnp.asarray(ek, BF), jnp.asarray(ev, BF), jnp.asarray(sel),
        jnp.asarray(kcol), jnp.asarray(qcol), row0, pool_lane,
    )


def kernel(
    n, heads, row0, pool_lane,
    tok_hbm, wq_hbm, wk_hbm, wv_hbm, wo_hbm, gain_ref, scale_ref, pq_ref,
    ek_ref, ev_ref, sel_ref, kcol_ref, qcol_ref,
    mixed_ref, pooled_ref,
    tok, wq, wk, wv, wo, halo, nrm, nrmq, kk, vv, qq, kaug, vaug, qaug, att, st, rc,
    load_sem, tok_send, tok_recv, st_send, st_recv,
):
    rows, cols, width = tok.shape
    pcols = cols + 2 * PAD
    steps = n.bit_length() - 1
    pairs = width // 128
    hw = width // heads
    blocks = cols // BLOCK
    krows = rows + 2 * RAD
    npq = pq_ref.shape[0]
    nt = 256 if width % 256 == 0 else 128
    me = lax.axis_index("row")

    loads = [
        pltpu.make_async_copy(src, dst, load_sem.at[i])
        for i, (src, dst) in enumerate(
            [(tok_hbm, tok), (wq_hbm, wq), (wk_hbm, wk), (wv_hbm, wv), (wo_hbm, wo)]
        )
    ]
    for load in loads:
        load.start()

    partners = [me + (1 - 2 * ((me // (1 << k)) % 2)) * (1 << k) for k in range(steps)]
    barrier = pltpu.get_barrier_semaphore()

    def signal(to):
        pl.semaphore_signal(barrier, inc=1, device_id={"row": to}, device_id_type=MESH)

    beside = lax.rem(me + n - 1 + 2 * (me % 2), n)
    for other in partners + [beside]:
        signal(other)
    pl.semaphore_wait(barrier, steps + 1)

    to_left = pltpu.make_async_remote_copy(
        tok_hbm.at[pl.ds(0, RAD)], halo.at[1], tok_send.at[0], tok_recv.at[1],
        device_id={"row": jnp.maximum(me - 1, 0)}, device_id_type=MESH)
    to_right = pltpu.make_async_remote_copy(
        tok_hbm.at[pl.ds(rows - RAD, RAD)], halo.at[0], tok_send.at[1], tok_recv.at[0],
        device_id={"row": jnp.minimum(me + 1, n - 1)}, device_id_type=MESH)
    pl.when(me > 0)(lambda: to_left.start())
    pl.when(me < n - 1)(lambda: to_right.start())

    lane = lax.broadcasted_iota(jnp.int32, (1, 128), 1)
    gain = gain_ref[...]

    def normalized(x):
        x = x.astype(F32)
        return x * lax.rsqrt(jnp.mean(x * x, axis=-1, keepdims=True) + EPS) * gain

    def padded(y):
        zero = jnp.zeros((PAD, y.shape[1]), F32)
        return jnp.concatenate([zero, y, zero], axis=0).astype(BF)

    def split(t, kind):
        hi = t.astype(BF).astype(F32)
        mid = (t - hi).astype(BF).astype(F32)
        low = t - hi - mid
        kind = sel_ref[kind : kind + 1, :]
        return jnp.where(kind == 0, hi, jnp.where(kind == 1, mid, jnp.where(kind == 2, low, 0.0)))

    def times(u, pick):
        u = u.astype(F32)
        sq = u * u
        hi = sq.astype(BF)
        low = (sq - hi.astype(F32)).astype(BF)
        total = jnp.dot(hi, pick, preferred_element_type=F32)
        total = total + jnp.dot(low, pick, preferred_element_type=F32)
        return jnp.sqrt(1.0 + total)

    def keys_values(first, count):
        flat = nrm[pl.ds(first, count)].reshape(count * pcols, width)

        def tile(j, _):
            part = pl.ds(pl.multiple_of(j * nt, nt), nt)
            k = jnp.dot(flat, wk[:, part], preferred_element_type=F32).astype(BF)
            kk[pl.ds(first, count), :, part] = k.reshape(count, pcols, nt)
            v = jnp.dot(flat, wv[:, part], preferred_element_type=F32).astype(BF)
            vv[pl.ds(first, count), :, part] = v.reshape(count, pcols, nt)
            return 0

        lax.fori_loop(0, width // nt, tile, 0)

        def aug(i, _):
            slot = first + i
            inside = jnp.logical_and(
                jnp.logical_or(slot >= RAD, me > 0), jnp.logical_or(slot < RAD + rows, me < n - 1))
            qrow = lane - row0
            seen = (qrow <= slot) & (qrow >= slot - 2 * RAD) & inside
            row_mask = jnp.where((qrow >= 0) & (qrow < rows) & ~seen, FAR, 0.0)
            kaug[slot] = (split(times(kk[slot], ek_ref[...]), 0) + row_mask + kcol_ref[...]).astype(BF)
            vaug[slot] = split(times(vv[slot], ev_ref[...]), 2).astype(BF)
            return 0

        lax.fori_loop(0, count, aug, 0)

    loads[0].wait()

    def own_norm(r, _):
        y = normalized(tok[r])
        nrmq[r] = y.astype(BF)
        nrm[RAD + r] = padded(y)
        return 0

    lax.fori_loop(0, rows, own_norm, 0)
    for load in loads[1:4]:
        load.wait()
    keys_values(RAD, rows)

    def query_tile(j, _):
        part = pl.ds(pl.multiple_of(j * nt, nt), nt)
        q = jnp.dot(nrmq[...].reshape(rows * cols, width), wq[:, part], preferred_element_type=F32)
        qq[:, :, part] = q.astype(BF).reshape(rows, cols, nt)
        return 0

    lax.fori_loop(0, width // nt, query_tile, 0)

    def query_aug(r, _):
        onehot = jnp.where(lane == row0 + r, 1.0, 0.0)
        qaug[r] = (qcol_ref[...] + onehot - split(times(qq[r], ek_ref[...]), 1)).astype(BF)
        return 0

    lax.fori_loop(0, rows, query_aug, 0)

    def head_pair(q, aug, p):
        zero = jnp.zeros((), BF)
        low = lane < hw
        out = []
        for i in range(2):
            h = 2 * p + i
            mine = low if i == 0 else ~low
            keep = ((lane >= 6 * h) & (lane < 6 * h + 6)) | (lane >= row0)
            out.append(jnp.concatenate(
                [jnp.where(mine, q, zero), jnp.where(keep, aug, zero)], axis=1))
        return jnp.concatenate(out, axis=0)

    pq_aug = (jnp.where(lane == pool_lane, 1.0, 0.0) - split(times(pq_ref[...], ek_ref[...]), 1)).astype(BF)

    own = pl.ds(RAD, rows)
    peaks = jnp.full((npq, 128), 0.0, F32)
    tsum = jnp.full((npq, 128), 1.0, F32)
    for p in range(pairs):
        part = pl.ds(128 * p, 128)
        keys = jnp.concatenate(
            [kk[own, :, part].reshape(rows * pcols, 128), kaug[own].reshape(rows * pcols, 128)], axis=1)
        vals = jnp.concatenate(
            [vv[own, :, part].reshape(rows * pcols, 128), vaug[own].reshape(rows * pcols, 128)], axis=1)
        d = lax.dot_general(head_pair(pq_ref[:, part], pq_aug, p), keys, NT, preferred_element_type=F32)
        top = jnp.max(d, axis=-1, keepdims=True)
        scaled = []
        for i in range(2):
            c = (2.0 * LOG2E) * scale_ref[2 * p + i]
            mine = slice(i * npq, (i + 1) * npq)
            scaled.append((d[mine] - top[mine]) * c)
            peaks = jnp.where(lane == 2 * p + i, top[mine] * c, peaks)
        f = jnp.exp2(jnp.concatenate(scaled, axis=0))
        hi = f.astype(BF)
        rest = f - hi.astype(F32)
        mid = rest.astype(BF)
        low = (rest - mid.astype(F32)).astype(BF)
        m = jnp.dot(jnp.concatenate([hi, mid, low], axis=0), vals, preferred_element_type=F32)
        m = m[: 2 * npq] + m[2 * npq : 4 * npq] + m[4 * npq :]
        st[0, :, part] = jnp.where(lane < hw, m[:npq, :128], m[npq:, :128])
        for i in range(2):
            h = 2 * p + i
            tv = jnp.where((lane >= 3 * h) & (lane < 3 * h + 3), m[i * npq : (i + 1) * npq, 128:], 0.0)
            tsum = jnp.where(lane == h, jnp.sum(tv, axis=-1, keepdims=True), tsum)
    st[0, :, width : width + 128] = peaks
    st[0, :, width + 128 : width + 256] = tsum

    swaps = [
        pltpu.make_async_remote_copy(
            st.at[k], rc.at[k], st_send.at[k], st_recv.at[k],
            device_id={"row": partners[k]}, device_id_type=MESH)
        for k in range(steps)
    ]
    swaps[0].start()

    def spread_heads(x, p):
        return jnp.where(lane < hw, x[:, 2 * p : 2 * p + 1], x[:, 2 * p + 1 : 2 * p + 2])

    def merge(k):
        swaps[k].wait()
        peak_mine, peak_other = st[k, :, width : width + 128], rc[k, :, width : width + 128]
        peak = jnp.maximum(peak_mine, peak_other)
        f_mine, f_other = jnp.exp2(peak_mine - peak), jnp.exp2(peak_other - peak)
        st[k + 1, :, width : width + 128] = peak
        tpart = pl.ds(width + 128, 128)
        st[k + 1, :, tpart] = st[k, :, tpart] * f_mine + rc[k, :, tpart] * f_other
        for p in range(pairs):
            part = pl.ds(128 * p, 128)
            a = st[k, :, part] * spread_heads(f_mine, p)
            b = rc[k, :, part] * spread_heads(f_other, p)
            st[k + 1, :, part] = a + b
        if k + 1 < steps:
            swaps[k + 1].start()

    def side(i, first, there):
        @pl.when(there)
        def _():
            (to_right if i == 0 else to_left).wait_recv()

        @pl.when(jnp.logical_not(there))
        def _():
            halo[i] = jnp.zeros(halo.shape[1:], BF)

        def norm(r, _):
            nrm[first + r] = padded(normalized(halo[i, r]))
            return 0

        lax.fori_loop(0, RAD, norm, 0)
        keys_values(first, RAD)

    side(0, 0, me > 0)
    side(1, RAD + rows, me < n - 1)

    def attend(p, _):
        part = pl.ds(pl.multiple_of(128 * p, 128), 128)
        c0 = (2.0 * LOG2E) * scale_ref[2 * p]
        c1 = (2.0 * LOG2E) * scale_ref[2 * p + 1]
        for b in range(blocks):
            qs, ks = pl.ds(b * BLOCK, BLOCK), pl.ds(b * BLOCK, WIN)
            nq, nk = rows * BLOCK, krows * WIN
            q = head_pair(qq[:, qs, part].reshape(nq, 128), qaug[:, qs, :].reshape(nq, 128), p)
            keys = jnp.concatenate(
                [kk[:, ks, part].reshape(nk, 128), kaug[:, ks, :].reshape(nk, 128)], axis=1)
            vals = jnp.concatenate(
                [vv[:, ks, part].reshape(nk, 128), vaug[:, ks, :].reshape(nk, 128)], axis=1)
            d = lax.dot_general(q, keys, NT, preferred_element_type=F32)
            d = d - jnp.max(d, axis=-1, keepdims=True)
            e = jnp.concatenate([jnp.exp2(d[:nq] * c0), jnp.exp2(d[nq:] * c1)], axis=0).astype(BF)
            m = jnp.dot(e, vals, preferred_element_type=F32)
            out = []
            for i in range(2):
                h = 2 * p + i
                sp, tv = m[i * nq : (i + 1) * nq, :128], m[i * nq : (i + 1) * nq, 128:]
                mine = (lane < hw) if i == 0 else (lane >= hw)
                mt = jnp.sum(jnp.where((lane >= 3 * h) & (lane < 3 * h + 3), tv, 0.0), axis=-1, keepdims=True)
                ss = jnp.sum(jnp.where(mine, sp * sp, 0.0), axis=-1, keepdims=True)
                out.append(sp * lax.rsqrt(mt * mt - ss))
            att[:, qs, part] = jnp.where(lane < hw, out[0], out[1]).astype(BF).reshape(rows, BLOCK, 128)
        for k in range(steps):
            pl.when(p == min(k, pairs - 1))(functools.partial(merge, k))
        return 0

    lax.fori_loop(0, pairs, attend, 0)

    last = st.at[steps]
    mt = last[:, width + 128 : width + 256]
    for p in range(pairs):
        part = pl.ds(128 * p, 128)
        sp = last[:, part]
        sq = sp * sp
        ss = jnp.where(
            lane < hw,
            jnp.sum(jnp.where(lane < hw, sq, 0.0), axis=-1, keepdims=True),
            jnp.sum(jnp.where(lane < hw, 0.0, sq), axis=-1, keepdims=True))
        t = spread_heads(mt, p)
        pooled_ref[:, part] = sp / jnp.sqrt(t * t - ss)

    loads[4].wait()

    def out_tile(j, _):
        part = pl.ds(pl.multiple_of(j * nt, nt), nt)
        y = jnp.dot(att[...].reshape(rows * cols, width), wo[:, part], preferred_element_type=F32)
        y = y + tok[:, :, part].reshape(rows * cols, nt).astype(F32)
        mixed_ref[:, :, part] = y.astype(BF).reshape(rows, cols, nt)
        return 0

    lax.fori_loop(0, width // nt, out_tile, 0)
    pl.when(me > 0)(lambda: to_left.wait_send())
    pl.when(me < n - 1)(lambda: to_right.wait_send())


def per_device(n, tokens, norm_gain, wq, wk, wv, wo, head_scale, pool_queries):
    rows, cols, width = tokens.shape
    heads = head_scale.shape[0]
    npq = pool_queries.shape[0]
    steps = n.bit_length() - 1
    assert n == 1 << steps and rows >= RAD and cols % BLOCK == 0 and 2 * width == 128 * heads
    ek, ev, sel, kcol, qcol, row0, pool_lane = tables(heads, width, rows, cols)
    krows, pcols = rows + 2 * RAD, cols + 2 * PAD
    vm = pl.BlockSpec(memory_space=pltpu.VMEM)
    hbm = pl.BlockSpec(memory_space=pl.ANY)
    V = pltpu.VMEM
    wshape = V((width, width), BF)
    return pl.pallas_call(
        functools.partial(kernel, n, heads, row0, pool_lane),
        out_shape=(
            jax.ShapeDtypeStruct(tokens.shape, BF),
            jax.ShapeDtypeStruct((npq, width), F32),
        ),
        in_specs=[hbm] * 5 + [vm, pl.BlockSpec(memory_space=pltpu.SMEM)] + [vm] * 6,
        out_specs=(vm, vm),
        scratch_shapes=[
            V(tokens.shape, BF), wshape, wshape, wshape, wshape,
            V((2, RAD, cols, width), BF),
            V((krows, pcols, width), BF),
            V(tokens.shape, BF),
            V((krows, pcols, width), BF),
            V((krows, pcols, width), BF),
            V(tokens.shape, BF),
            V((krows, pcols, 128), BF),
            V((krows, pcols, 128), BF),
            V((rows, cols, 128), BF),
            V(tokens.shape, BF),
            V((steps + 1, npq, width + 256), F32),
            V((steps, npq, width + 256), F32),
            pltpu.SemaphoreType.DMA((5,)),
            pltpu.SemaphoreType.DMA((2,)),
            pltpu.SemaphoreType.DMA((2,)),
            pltpu.SemaphoreType.DMA((steps,)),
            pltpu.SemaphoreType.DMA((steps,)),
        ],
        compiler_params=pltpu.CompilerParams(
            collective_id=0, has_side_effects=True, vmem_limit_bytes=48 * 1024 * 1024),
    )(tokens, wq, wk, wv, wo, norm_gain.reshape(1, width), head_scale, pool_queries, ek, ev, sel, kcol, qcol)


def solution(mesh):
    placed = (P(("slide", "row"), None, None), P(), P(), P(), P(), P(), P(), P())
    return jax.shard_map(
        functools.partial(per_device, mesh.shape["row"]),
        mesh=mesh,
        in_specs=placed,
        out_specs=(P(("slide", "row"), None, None), P("slide", None)),
        check_vma=False,
    )
```

time: 233 us -> 62.1 us (0.27)
  blocking collectives: 87 us -> 0 us
  local copies, waits for them, and re-layouts: 86.1 us -> 12.8 us
  Pallas kernels: 0 us -> 48.1 us
  other arithmetic: 34.2 us -> 0 us
  matrix products: 16.9 us -> 0 us
  starting transfers between devices: 5.49 us -> 0 us
    all_gather x3 -> x0, blocking collectives: 87 us -> none  [merged_2(): everything = jax.tree.map(lambda part: lax.all_gather(part, axis), shard)]
    pallas_call x0 -> x1, Pallas kernels: none -> 48.1 us  [per_device(): pl.pallas_call(functools.partial(kernel, n, heads, row0, pool_lane), out_...]
    slice x15 -> x0, local copies, waits for them, and re-layouts: 21.4 us -> none  [the longest x6 16.8 us: split_cols(): main_part = array[..., :group].reshape(lead + (blocks, block))]
    dot_general x8 -> x0, matrix products: 16.9 us -> none  [the longest x3 6.92 us: project(): lax.dot_general(weight, flattened, (((0,), (1,)), ((), ())), preferred_el...]
    reduce_sum x9 -> x0, other arithmetic: 15.4 us -> none  [the longest x1 7.33 us: one_tile(): jnp.sum(weights.astype(jnp.float32) * vtime_blocks[:, :, None, :], axis=-1)]
    dynamic_slice x15 -> x0, local copies, waits for them, and re-layouts: 13.7 us -> none  [hop(): return combine(so_far, jax.tree.map(lambda part: part[k], everything))]
    transpose x7 -> x0, local copies, waits for them, and re-layouts: 8.94 us -> none  [the longest x1 3.64 us: one_tile(): key_blocks = split_cols(key_pad, group, block, RAD).transpose(0, 3, 1, 2, 4)]
    transpose x4 -> x0, other arithmetic: 8.44 us -> none  [the longest x1 4.08 us: one_tile(): split_cols(value_pad, group, block, RAD).transpose(0, 3, 1, 2, 4)]
  transfers between devices with their start and end apart: 2 -> 0, of which waited for: 0 -> 0; matrix products, arithmetic and copies ran while one was open for 13% -> 0% of each run, Pallas kernels for 0% -> 0%
where the time goes in v1:
time: 62.1 us; the launch traced here: 61.6 us
  Pallas kernels  48.1 us (77%)
  local copies, waits for them, and re-layouts  12.8 us (21%)
  between operations  0.65 us (1%)
    pallas_call x1, Pallas kernels, per_device(): pl.pallas_call(functools.partial(kernel, n, heads, row0, pool_lane), out_...  48.1 us
    unnamed x24, local copies, waits for them, and re-layouts  12.1 us

profile of v1, /device:TPU:0, one launch (start us, length us, event | category | flops | bytes accessed | tf_op | source)
XLA Modules:
  0.0 61.6 jit_solution(16405235148636290404)
XLA Ops:
  0.6 0.7 %reshape.7.gain_ref = f32[1,768]{1,0:T(1,128)S(1)} reshape(f32[768]{0:T(1024)} %param.14) | data formatting | bytes 6144 | tf_op jit(solution)/shard_map/reshape | solution.py:376
  1.3 0.0 copy-start
  1.3 1.3 %copy-done = bf16[768,768]{1,0:T(8,128)(2,1)S(1)} copy-done((bf16[768,768]{1,0:T(8,128)(2,1)S(1)}, bf16[768,768]{1,0:T(8,128)(2,1)}, u32[]{:S(2)}) %copy-start) | copy-done | bytes 1179672
  2.6 0.0 copy-start.1
  2.6 1.3 %copy-done.1 = bf16[768,768]{1,0:T(8,128)(2,1)S(1)} copy-done((bf16[768,768]{1,0:T(8,128)(2,1)S(1)}, bf16[768,768]{1,0:T(8,128)(2,1)}, u32[]{:S(2)}) %copy-start.1) | copy-done | bytes 1179672
  3.9 0.0 copy-start.2
  3.9 1.3 %copy-done.2 = bf16[768,768]{1,0:T(8,128)(2,1)S(1)} copy-done((bf16[768,768]{1,0:T(8,128)(2,1)S(1)}, bf16[768,768]{1,0:T(8,128)(2,1)}, u32[]{:S(2)}) %copy-start.2) | copy-done | bytes 1179672
  5.1 0.0 copy-start.3
  5.1 1.1 %copy-done.3 = bf16[4,128,768]{2,1,0:T(8,128)(2,1)S(1)} copy-done((bf16[4,128,768]{2,1,0:T(8,128)(2,1)S(1)}, bf16[4,128,768]{2,1,0:T(8,128)(2,1)}, u32[]{:S(2)}) %copy-start.3) | copy-done | bytes 786456
  6.3 0.0 copy-start.4
  6.3 0.9 %copy-done.4 = bf16[768,128]{1,0:T(8,128)(2,1)S(1)} copy-done((bf16[768,128]{1,0:T(8,128)(2,1)S(1)}, bf16[768,128]{1,0:T(8,128)(2,1)}, u32[]{:S(2)}) %copy-start.4) | copy-done | bytes 196632
  7.2 0.0 copy-start.5
  7.2 0.9 %copy-done.5 = bf16[768,128]{1,0:T(8,128)(2,1)S(1)} copy-done((bf16[768,128]{1,0:T(8,128)(2,1)S(1)}, bf16[768,128]{1,0:T(8,128)(2,1)}, u32[]{:S(2)}) %copy-start.5) | copy-done | bytes 196632
  8.1 0.0 copy-start.6
  8.1 0.9 %copy-done.6 = f32[144,128]{1,0:T(8,128)S(1)} copy-done((f32[144,128]{1,0:T(8,128)S(1)}, f32[144,128]{1,0:T(8,128)}, u32[]{:S(2)}) %copy-start.6) | copy-done | bytes 73752
  9.0 0.0 copy-start.7
  9.0 0.8 %copy-done.7 = f32[128,128]{1,0:T(8,128)S(1)} copy-done((f32[128,128]{1,0:T(8,128)S(1)}, f32[128,128]{1,0:T(8,128)}, u32[]{:S(2)}) %copy-start.7) | copy-done | bytes 65560
  9.8 0.0 copy-start.8
  9.8 0.7 %copy-done.8 = bf16[16,768]{1,0:T(8,128)(2,1)S(1)} copy-done((bf16[16,768]{1,0:T(8,128)(2,1)S(1)}, bf16[16,768]{1,0:T(8,128)(2,1)}, u32[]{:S(2)}) %copy-start.8) | copy-done | bytes 24600
  10.6 0.0 copy-start.9
  10.6 0.7 %copy-done.9 = f32[8,128]{1,0:T(8,128)S(1)} copy-done((f32[8,128]{1,0:T(8,128)S(1)}, f32[8,128]{1,0:T(8,128)}, u32[]{:S(2)}) %copy-start.9) | copy-done | bytes 4120
  11.3 0.0 copy-start.10
  11.3 0.7 %copy-done.10 = f32[12]{0:T(128)S(1)} copy-done((f32[12]{0:T(128)S(1)}, f32[12]{0:T(128)}, u32[]{:S(2)}) %copy-start.10) | copy-done | bytes 72
  11.9 48.1 %shard_map.140 = (bf16[4,128,768]{2,1,0:T(8,128)(2,1)S(1)}, f32[16,768]{1,0:T(8,128)S(1)}) custom-call(bf16[4,128,768]{2,1,0:T(8,128)(2,1)S(1)} %copy-done.3, bf16[768,768]{1,0:T(8,128)(2,1)S(1)} %copy-done, bf16[768,768]{1,0:T(8,128)(2,1)S(1)} %copy-done.1, bf16[768,768]{1,0:T(8,128)(2,1)S(1)} %copy-done.2, bf16[768,768]{1,0:T(8,128)(2,1)} %wo_hbm.1, ...), custom_call_target="tpu_custom_call" | custom-call | tf_op jit(solution)/shard_map/pallas_call | solution.py:346
  60.1 0.9 %copy.17 = bf16[4,128,768]{2,1,0:T(8,128)(2,1)} copy(bf16[4,128,768]{2,1,0:T(8,128)(2,1)S(1)} %get-tuple-element.4) | data formatting | bytes 1572864
  61.0 0.6 %copy.18 = f32[16,768]{1,0:T(8,128)} copy(f32[16,768]{1,0:T(8,128)S(1)} %get-tuple-element.5) | data formatting | bytes 98304
Async XLA Ops:
  1.3 1.3 %copy-start = (bf16[768,768]{1,0:T(8,128)(2,1)S(1)}, bf16[768,768]{1,0:T(8,128)(2,1)}, u32[]{:S(2)}) copy-start(bf16[768,768]{1,0:T(8,128)(2,1)} %wq_hbm.1) | copy-start | bytes 3538948
  2.6 1.3 %copy-start.1 = (bf16[768,768]{1,0:T(8,128)(2,1)S(1)}, bf16[768,768]{1,0:T(8,128)(2,1)}, u32[]{:S(2)}) copy-start(bf16[768,768]{1,0:T(8,128)(2,1)} %wk_hbm.1) | copy-start | bytes 3538948
  3.9 1.3 %copy-start.2 = (bf16[768,768]{1,0:T(8,128)(2,1)S(1)}, bf16[768,768]{1,0:T(8,128)(2,1)}, u32[]{:S(2)}) copy-start(bf16[768,768]{1,0:T(8,128)(2,1)} %wv_hbm.1) | copy-start | bytes 3538948
  5.1 1.1 %copy-start.3 = (bf16[4,128,768]{2,1,0:T(8,128)(2,1)S(1)}, bf16[4,128,768]{2,1,0:T(8,128)(2,1)}, u32[]{:S(2)}) copy-start(bf16[4,128,768]{2,1,0:T(8,128)(2,1)} %tok_hbm.1) | copy-start | bytes 2359300
  6.3 0.9 %copy-start.4 = (bf16[768,128]{1,0:T(8,128)(2,1)S(1)}, bf16[768,128]{1,0:T(8,128)(2,1)}, u32[]{:S(2)}) copy-start(bf16[768,128]{1,0:T(8,128)(2,1)} %constant.11.clone.ev_ref) | copy-start | bytes 589828
  7.2 0.9 %copy-start.5 = (bf16[768,128]{1,0:T(8,128)(2,1)S(1)}, bf16[768,128]{1,0:T(8,128)(2,1)}, u32[]{:S(2)}) copy-start(bf16[768,128]{1,0:T(8,128)(2,1)} %constant.10.clone.ek_ref) | copy-start | bytes 589828
  8.1 0.9 %copy-start.6 = (f32[144,128]{1,0:T(8,128)S(1)}, f32[144,128]{1,0:T(8,128)}, u32[]{:S(2)}) copy-start(f32[144,128]{1,0:T(8,128)} %constant.13.clone.kcol_ref) | copy-start | bytes 221188
  9.0 0.8 %copy-start.7 = (f32[128,128]{1,0:T(8,128)S(1)}, f32[128,128]{1,0:T(8,128)}, u32[]{:S(2)}) copy-start(f32[128,128]{1,0:T(8,128)} %constant.14.clone.qcol_ref) | copy-start | bytes 196612
  9.8 0.7 %copy-start.8 = (bf16[16,768]{1,0:T(8,128)(2,1)S(1)}, bf16[16,768]{1,0:T(8,128)(2,1)}, u32[]{:S(2)}) copy-start(bf16[16,768]{1,0:T(8,128)(2,1)} %pq_ref.1) | copy-start | bytes 73732
  10.6 0.7 %copy-start.9 = (f32[8,128]{1,0:T(8,128)S(1)}, f32[8,128]{1,0:T(8,128)}, u32[]{:S(2)}) copy-start(f32[8,128]{1,0:T(8,128)} %constant.12.clone.sel_ref) | copy-start | bytes 12292
  11.3 0.7 %copy-start.10 = (f32[12]{0:T(128)S(1)}, f32[12]{0:T(128)}, u32[]{:S(2)}) copy-start(f32[12]{0:T(128)} %scale_ref.1) | copy-start | bytes 148

commit v2 on v1

--- a/solution.py
+++ b/solution.py
@@ -47,17 +47,16 @@
     qcol = np.zeros((cols, 128), np.float32)
     qcol[np.arange(cols), col0 + np.arange(cols) % RING] = 1.0
     return (
-        jnp.asarray(ek, BF), jnp.asarray(ev, BF), jnp.asarray(sel),
-        jnp.asarray(kcol), jnp.asarray(qcol), row0, pool_lane,
+        jnp.asarray(np.stack([ek, ev]), BF), jnp.asarray(np.concatenate([sel, kcol, qcol])),
+        row0, pool_lane,
     )
 
 
 def kernel(
     n, heads, row0, pool_lane,
-    tok_hbm, wq_hbm, wk_hbm, wv_hbm, wo_hbm, gain_ref, scale_ref, pq_ref,
-    ek_ref, ev_ref, sel_ref, kcol_ref, qcol_ref,
+    tok_hbm, wq_hbm, wk_hbm, wv_hbm, wo_hbm, pick_hbm, table_hbm, pq_hbm, gain_ref, scale_ref,
     mixed_ref, pooled_ref,
-    tok, wq, wk, wv, wo, halo, nrm, nrmq, kk, vv, qq, kaug, vaug, qaug, att, st, rc,
+    tok, wq, wk, wv, wo, picks, table, pq_ref, halo, nrm, nrmq, kk, vv, qq, kaug, vaug, qaug, att, st, rc,
     load_sem, tok_send, tok_recv, st_send, st_recv,
 ):
     rows, cols, width = tok.shape
@@ -68,13 +67,17 @@
     blocks = cols // BLOCK
     krows = rows + 2 * RAD
     npq = pq_ref.shape[0]
+    ek_ref, ev_ref = picks.at[0], picks.at[1]
+    sel_ref = table.at[pl.ds(0, 8)]
+    kcol_ref = table.at[pl.ds(8, pcols)]
+    qcol_ref = table.at[pl.ds(8 + pcols, cols)]
     nt = 256 if width % 256 == 0 else 128
     me = lax.axis_index("row")
 
     loads = [
         pltpu.make_async_copy(src, dst, load_sem.at[i])
         for i, (src, dst) in enumerate(
-            [(tok_hbm, tok), (wq_hbm, wq), (wk_hbm, wk), (wv_hbm, wv), (wo_hbm, wo)]
+            [(tok_hbm, tok), (wk_hbm, wk), (wv_hbm, wv), (pick_hbm, picks), (table_hbm, table), (pq_hbm, pq_ref), (wq_hbm, wq), (wo_hbm, wo)]
         )
     ]
     for load in loads:
@@ -97,11 +100,13 @@
     to_right = pltpu.make_async_remote_copy(
         tok_hbm.at[pl.ds(rows - RAD, RAD)], halo.at[0], tok_send.at[1], tok_recv.at[0],
         device_id={"row": jnp.minimum(me + 1, n - 1)}, device_id_type=MESH)
-    pl.when(me > 0)(lambda: to_left.start())
+    even = me % 2 == 0
+    pl.when(jnp.logical_and(even, me > 0))(lambda: to_left.start())
     pl.when(me < n - 1)(lambda: to_right.start())
+    pl.when(jnp.logical_not(even))(lambda: to_left.start())
 
     lane = lax.broadcasted_iota(jnp.int32, (1, 128), 1)
-    gain = gain_ref[...]
+    gain = gain_ref[...].reshape(1, width)
 
     def normalized(x):
         x = x.astype(F32)
@@ -162,24 +167,9 @@
         return 0
 
     lax.fori_loop(0, rows, own_norm, 0)
-    for load in loads[1:4]:
+    for load in loads[1:6]:
         load.wait()
     keys_values(RAD, rows)
-
-    def query_tile(j, _):
-        part = pl.ds(pl.multiple_of(j * nt, nt), nt)
-        q = jnp.dot(nrmq[...].reshape(rows * cols, width), wq[:, part], preferred_element_type=F32)
-        qq[:, :, part] = q.astype(BF).reshape(rows, cols, nt)
-        return 0
-
-    lax.fori_loop(0, width // nt, query_tile, 0)
-
-    def query_aug(r, _):
-        onehot = jnp.where(lane == row0 + r, 1.0, 0.0)
-        qaug[r] = (qcol_ref[...] + onehot - split(times(qq[r], ek_ref[...]), 1)).astype(BF)
-        return 0
-
-    lax.fori_loop(0, rows, query_aug, 0)
 
     def head_pair(q, aug, p):
         zero = jnp.zeros((), BF)
@@ -254,15 +244,31 @@
         if k + 1 < steps:
             swaps[k + 1].start()
 
-    def side(i, first, there):
-        @pl.when(there)
-        def _():
-            (to_right if i == 0 else to_left).wait_recv()
-
-        @pl.when(jnp.logical_not(there))
-        def _():
-            halo[i] = jnp.zeros(halo.shape[1:], BF)
-
+    loads[6].wait()
+
+    def query_tile(j, _):
+        part = pl.ds(pl.multiple_of(j * nt, nt), nt)
+        q = jnp.dot(nrmq[...].reshape(rows * cols, width), wq[:, part], preferred_element_type=F32)
+        qq[:, :, part] = q.astype(BF).reshape(rows, cols, nt)
+        return 0
+
+    lax.fori_loop(0, width // nt, query_tile, 0)
+
+    def query_aug(r, _):
+        onehot = jnp.where(lane == row0 + r, 1.0, 0.0)
+        qaug[r] = (qcol_ref[...] + onehot - split(times(qq[r], ek_ref[...]), 1)).astype(BF)
+        return 0
+
+    lax.fori_loop(0, rows, query_aug, 0)
+
+    merge(0)
+
+    def arrived(i):
+        pltpu.make_async_remote_copy(
+            tok_hbm.at[pl.ds(0, RAD)], halo.at[i], tok_send.at[i], tok_recv.at[i],
+            device_id={"row": beside}, device_id_type=MESH).wait_recv()
+
+    def side_rows(i, first):
         def norm(r, _):
             nrm[first + r] = padded(normalized(halo[i, r]))
             return 0
@@ -270,8 +276,22 @@
         lax.fori_loop(0, RAD, norm, 0)
         keys_values(first, RAD)
 
-    side(0, 0, me > 0)
-    side(1, RAD + rows, me < n - 1)
+    near, far = 1 - me % 2, me % 2
+    inner = jnp.logical_and(me > 0, me < n - 1)
+    arrived(near)
+    side_rows(near, near * (RAD + rows))
+    for k in range(1, min(steps, 3)):
+        merge(k)
+
+    @pl.when(inner)
+    def _():
+        arrived(far)
+
+    @pl.when(jnp.logical_not(inner))
+    def _():
+        halo[far] = jnp.zeros(halo.shape[1:], BF)
+
+    side_rows(far, far * (RAD + rows))
 
     def attend(p, _):
         part = pl.ds(pl.multiple_of(128 * p, 128), 128)
@@ -298,8 +318,8 @@
                 ss = jnp.sum(jnp.where(mine, sp * sp, 0.0), axis=-1, keepdims=True)
                 out.append(sp * lax.rsqrt(mt * mt - ss))
             att[:, qs, part] = jnp.where(lane < hw, out[0], out[1]).astype(BF).reshape(rows, BLOCK, 128)
-        for k in range(steps):
-            pl.when(p == min(k, pairs - 1))(functools.partial(merge, k))
+        for k in range(3, steps):
+            pl.when(p == min(k - 3, pairs - 1))(functools.partial(merge, k))
         return 0
 
     lax.fori_loop(0, pairs, attend, 0)
@@ -317,7 +337,7 @@
         t = spread_heads(mt, p)
         pooled_ref[:, part] = sp / jnp.sqrt(t * t - ss)
 
-    loads[4].wait()
+    loads[7].wait()
 
     def out_tile(j, _):
         part = pl.ds(pl.multiple_of(j * nt, nt), nt)
@@ -337,10 +357,10 @@
     npq = pool_queries.shape[0]
     steps = n.bit_length() - 1
     assert n == 1 << steps and rows >= RAD and cols % BLOCK == 0 and 2 * width == 128 * heads
-    ek, ev, sel, kcol, qcol, row0, pool_lane = tables(heads, width, rows, cols)
+    pick, table, row0, pool_lane = tables(heads, width, rows, cols)
     krows, pcols = rows + 2 * RAD, cols + 2 * PAD
     vm = pl.BlockSpec(memory_space=pltpu.VMEM)
-    hbm = pl.BlockSpec(memory_space=pl.ANY)
+    hbm = pl.BlockSpec(memory_space=pltpu.HBM)
     V = pltpu.VMEM
     wshape = V((width, width), BF)
     return pl.pallas_call(
@@ -349,10 +369,11 @@
             jax.ShapeDtypeStruct(tokens.shape, BF),
             jax.ShapeDtypeStruct((npq, width), F32),
         ),
-        in_specs=[hbm] * 5 + [vm, pl.BlockSpec(memory_space=pltpu.SMEM)] + [vm] * 6,
+        in_specs=[hbm] * 8 + [vm, pl.BlockSpec(memory_space=pltpu.SMEM)],
         out_specs=(vm, vm),
         scratch_shapes=[
             V(tokens.shape, BF), wshape, wshape, wshape, wshape,
+            V(pick.shape, BF), V(table.shape, F32), V(pool_queries.shape, BF),
             V((2, RAD, cols, width), BF),
             V((krows, pcols, width), BF),
             V(tokens.shape, BF),
@@ -365,15 +386,15 @@
             V(tokens.shape, BF),
             V((steps + 1, npq, width + 256), F32),
             V((steps, npq, width + 256), F32),
-            pltpu.SemaphoreType.DMA((5,)),
+            pltpu.SemaphoreType.DMA((8,)),
             pltpu.SemaphoreType.DMA((2,)),
             pltpu.SemaphoreType.DMA((2,)),
             pltpu.SemaphoreType.DMA((steps,)),
             pltpu.SemaphoreType.DMA((steps,)),
         ],
         compiler_params=pltpu.CompilerParams(
-            collective_id=0, has_side_effects=True, vmem_limit_bytes=48 * 1024 * 1024),
-    )(tokens, wq, wk, wv, wo, norm_gain.reshape(1, width), head_scale, pool_queries, ek, ev, sel, kcol, qcol)
+            collective_id=0, has_side_effects=True, vmem_limit_bytes=63 * 1024 * 1024),
+    )(tokens, wq, wk, wv, wo, pick, table, pool_queries, norm_gain, head_scale)
 
 
 def solution(mesh):

time: 62.1 us -> 49.1 us (0.79)
  local copies, waits for them, and re-layouts: 12.8 us -> 2.7 us
  Pallas kernels: 48.1 us -> 45.5 us
    unnamed x24 -> x4, local copies, waits for them, and re-layouts: 12.1 us -> 2.7 us
    pallas_call x1, Pallas kernels: 48.1 us -> 45.5 us  [per_device(): pl.pallas_call(functools.partial(kernel, n, heads, row0, pool_lane), out_...]
    reshape x1 -> x0, local copies, waits for them, and re-layouts: 0.69 us -> none  [per_device(): norm_gain.reshape(1, width)]
where the time goes in v2:
time: 49.1 us; the launch traced here: 48.9 us
  Pallas kernels  45.5 us (93%)
  local copies, waits for them, and re-layouts  2.7 us (5%)
  between operations  0.65 us (1%)
    pallas_call x1, Pallas kernels, per_device(): pl.pallas_call(functools.partial(kernel, n, heads, row0, pool_lane), out_...  45.5 us
    unnamed x4, local copies, waits for them, and re-layouts  2.7 us

profile of v2, /device:TPU:0, one launch (start us, length us, event | category | flops | bytes accessed | tf_op | source)
XLA Modules:
  0.0 48.9 jit_solution(3397111847189569336)
XLA Ops:
  0.6 45.5 %shard_map.113 = (bf16[4,128,768]{2,1,0:T(8,128)(2,1)}, f32[16,768]{1,0:T(8,128)}) custom-call(bf16[4,128,768]{2,1,0:T(8,128)(2,1)} %tok_hbm.1, bf16[768,768]{1,0:T(8,128)(2,1)} %wq_hbm.1, bf16[768,768]{1,0:T(8,128)(2,1)} %wk_hbm.1, bf16[768,768]{1,0:T(8,128)(2,1)} %wv_hbm.1, bf16[768,768]{1,0:T(8,128)(2,1)} %wo_hbm.1, ...), custom_call_target="tpu_custom_call" | custom-call | tf_op jit(solution)/shard_map/pallas_call | solution.py:366
  46.2 0.0 copy-start
  46.2 2.1 %copy.14 = bf16[4,128,768]{2,1,0:T(8,128)(2,1)} copy(bf16[4,128,768]{2,1,0:T(8,128)(2,1)} %get-tuple-element.4) | data formatting | bytes 1572864
  48.3 0.0 copy-done
  48.3 0.6 %copy.15 = f32[16,768]{1,0:T(8,128)} copy(f32[16,768]{1,0:T(8,128)S(1)} %copy-done) | data formatting | bytes 98304
Async XLA Ops:
  46.2 2.1 %copy-start = (f32[16,768]{1,0:T(8,128)S(1)}, f32[16,768]{1,0:T(8,128)}, u32[]{:S(2)}) copy-start(f32[16,768]{1,0:T(8,128)} %get-tuple-element.5) | copy-start | bytes 147460

commit v3 on v2

--- a/solution.py
+++ b/solution.py
@@ -280,8 +280,6 @@
     inner = jnp.logical_and(me > 0, me < n - 1)
     arrived(near)
     side_rows(near, near * (RAD + rows))
-    for k in range(1, min(steps, 3)):
-        merge(k)
 
     @pl.when(inner)
     def _():
@@ -318,8 +316,8 @@
                 ss = jnp.sum(jnp.where(mine, sp * sp, 0.0), axis=-1, keepdims=True)
                 out.append(sp * lax.rsqrt(mt * mt - ss))
             att[:, qs, part] = jnp.where(lane < hw, out[0], out[1]).astype(BF).reshape(rows, BLOCK, 128)
-        for k in range(3, steps):
-            pl.when(p == min(k - 3, pairs - 1))(functools.partial(merge, k))
+        for k in range(1, steps):
+            pl.when(p == (k - 1) * pairs // max(steps - 1, 1))(functools.partial(merge, k))
         return 0
 
     lax.fori_loop(0, pairs, attend, 0)

time: 49.1 us -> 45.2 us (0.921)
  the two profiles are of different devices: /device:TPU:0 before, /device:TPU:1 now
where the time goes in v3:
time: 45.2 us; the launch traced here: 45.1 us
  Pallas kernels  41.7 us (92%)
  local copies, waits for them, and re-layouts  2.7 us (6%)
  between operations  0.65 us (1%)
    pallas_call x1, Pallas kernels, per_device(): pl.pallas_call(functools.partial(kernel, n, heads, row0, pool_lane), out_...  41.7 us
    unnamed x4, local copies, waits for them, and re-layouts  2.7 us

profile of v3, /device:TPU:1, one launch (start us, length us, event | category | flops | bytes accessed | tf_op | source)
XLA Modules:
  0.0 45.1 jit_solution(4734942462104702757)
XLA Ops:
  0.6 41.7 %shard_map.113 = (bf16[4,128,768]{2,1,0:T(8,128)(2,1)}, f32[16,768]{1,0:T(8,128)}) custom-call(bf16[4,128,768]{2,1,0:T(8,128)(2,1)} %tok_hbm.1, bf16[768,768]{1,0:T(8,128)(2,1)} %wq_hbm.1, bf16[768,768]{1,0:T(8,128)(2,1)} %wk_hbm.1, bf16[768,768]{1,0:T(8,128)(2,1)} %wv_hbm.1, bf16[768,768]{1,0:T(8,128)(2,1)} %wo_hbm.1, ...), custom_call_target="tpu_custom_call" | custom-call | tf_op jit(solution)/shard_map/pallas_call | solution.py:364
  42.3 0.0 copy-start
  42.4 2.1 %copy.14 = bf16[4,128,768]{2,1,0:T(8,128)(2,1)} copy(bf16[4,128,768]{2,1,0:T(8,128)(2,1)} %get-tuple-element.4) | data formatting | bytes 1572864
  44.4 0.0 copy-done
  44.4 0.6 %copy.15 = f32[16,768]{1,0:T(8,128)} copy(f32[16,768]{1,0:T(8,128)S(1)} %copy-done) | data formatting | bytes 98304
Async XLA Ops:
  42.3 2.1 %copy-start = (f32[16,768]{1,0:T(8,128)S(1)}, f32[16,768]{1,0:T(8,128)}, u32[]{:S(2)}) copy-start(f32[16,768]{1,0:T(8,128)} %get-tuple-element.5) | copy-start | bytes 147460
